TPU v7x, 32 devices: a whole 2x2x4 slice. The times are simulated.
32 devices in a mesh: dp: 4 (over z), ctx: 4 (over x, core), fsdp: 2 (over y).
Axes of the slice: x: 2, y: 2, z: 4, core: 2. Of those that a mesh axis runs over, the one named last changes fastest.
Arguments:
- hidden: bfloat16 [8, 1024, 2048], P(('dp', 'fsdp'), 'ctx'), may hold values from -6 to 6
- segment_ids: int32 [8, 1024], P(('dp', 'fsdp')), may hold values from 0 to 4, as said below
- positions: int32 [8, 1024], P(('dp', 'fsdp')), may hold values from 0 to 799, as said below
- attn_gain: bfloat16 [2048], P(('dp', 'ctx', 'fsdp')), may hold values from 0.099609375 to 1.8984375
- w_query: bfloat16 [2048, 2048], P(('dp', 'fsdp'), 'ctx'), may hold values from -0.015625 to 0.015625
- w_key: bfloat16 [2048, 2048], P(('dp', 'fsdp'), 'ctx'), may hold values from -0.125 to 0.125
- w_value: bfloat16 [2048, 2048], P(('dp', 'fsdp'), 'ctx'), may hold values from -0.125 to 0.125
- w_attn_out: bfloat16 [2048, 2048], P('ctx', ('dp', 'fsdp')), may hold values from -1.5 to 1.5
- rel_table: bfloat16 [1024], P(('dp', 'ctx', 'fsdp')), may hold values from -4 to 4
- ffn_gain: bfloat16 [2048], P(('dp', 'ctx', 'fsdp')), may hold values from 0.099609375 to 1.8984375
- w_gate: bfloat16 [2048, 5120], P(('dp', 'fsdp'), 'ctx'), may hold values from -0.125 to 0.125
- w_up: bfloat16 [2048, 5120], P(('dp', 'fsdp'), 'ctx'), may hold values from -0.125 to 0.125
- w_down: bfloat16 [5120, 2048], P('ctx', ('dp', 'fsdp')), may hold values from -0.078125 to 0.078125
- cotangent: bfloat16 [8, 1024, 2048], P(('dp', 'fsdp'), 'ctx'), may hold values from -6 to 6
Outputs:
- output: bfloat16 [8, 1024, 2048], P(('dp', 'fsdp'), 'ctx')
- grad_hidden: float32 [8, 1024, 2048], P(('dp', 'fsdp'), 'ctx')
- grad_attn_gain: float32 [2048], P(('dp', 'ctx', 'fsdp'))
- grad_query: float32 [2048, 2048], P(('dp', 'fsdp'), 'ctx')
- grad_key: float32 [2048, 2048], P(('dp', 'fsdp'), 'ctx')
- grad_value: float32 [2048, 2048], P(('dp', 'fsdp'), 'ctx')
- grad_attn_out: float32 [2048, 2048], P('ctx', ('dp', 'fsdp'))
- bias_table_gradient: float32 [1024], P(('dp', 'ctx', 'fsdp'))
- grad_ffn_gain: float32 [2048], P(('dp', 'ctx', 'fsdp'))
- grad_gate: float32 [2048, 5120], P(('dp', 'fsdp'), 'ctx')
- grad_up: float32 [2048, 5120], P(('dp', 'fsdp'), 'ctx')
- grad_down: float32 [5120, 2048], P('ctx', ('dp', 'fsdp'))
Inputs may be any that keep to these rules, and one draw needn't show every extreme that they name: `segment_ids`: within each sequence the ids number its documents from 0 and never fall. One document of each sequence, its first or its second, holds exactly 800 tokens; every other document holds 60 to 800 tokens, except the last one, which the end of the sequence may cut short. `positions`: 0 at a document's first token and rising by one along it, consistent with segment_ids.
All inputs are finite; a program needn't handle non-finite values.
Results may differ from a plain program's by a relative error of at most 0.018.
Values may be sent and summed in bfloat16 or wider, within the bound.
A program may use at most 256 MiB of HBM per device.

v0:
```python
import jax
import jax.numpy as jnp
from jax import lax
from jax.sharding import PartitionSpec as P

H = 32
DH = 64
NB = 32
QB = 512
EPSILON = 1e-06
THRESHOLDS = (12, 16, 23, 32, 46, 64, 91)
MASKED = -1e30


def rms_norm(values, gain):
    return values * lax.rsqrt(jnp.mean(values * values, axis=-1, keepdims=True) + EPSILON) * gain


def gelu_tanh(values):
    return (
        0.5
        * values
        * (1.0 + jnp.tanh(0.7978845608028654 * (values + 0.044715 * values * values * values)))
    )


def bucket_table(query_pos, key_pos):
    relative = key_pos[None, :] - query_pos[:, None]
    distance = jnp.abs(relative)
    log_bucket = 8 + sum(((distance >= threshold).astype(jnp.int32) for threshold in THRESHOLDS))
    bucket = jnp.where(distance < 8, distance, log_bucket)
    return bucket + 16 * (relative > 0).astype(jnp.int32)


def gather_attention(w_query, w_key, w_value, w_attn_out):
    return (
        lax.all_gather(w_query, ("dp", "fsdp"), axis=0, tiled=True),
        lax.all_gather(w_key, ("dp", "fsdp"), axis=0, tiled=True),
        lax.all_gather(w_value, ("dp", "fsdp"), axis=0, tiled=True),
        lax.all_gather(w_attn_out, ("dp", "fsdp"), axis=1, tiled=True),
    )


def gather_feedforward(w_gate, w_up, w_down):
    return (
        lax.all_gather(w_gate, ("dp", "fsdp"), axis=0, tiled=True),
        lax.all_gather(w_up, ("dp", "fsdp"), axis=0, tiled=True),
        lax.all_gather(w_down, ("dp", "fsdp"), axis=1, tiled=True),
    )


def block_masks(segment_row, position_row, start):
    query_pos = lax.dynamic_slice_in_dim(position_row, start, QB)
    query_seg = lax.dynamic_slice_in_dim(segment_row, start, QB)
    buckets = bucket_table(query_pos, position_row)
    one_hot = (buckets[None] == jnp.arange(NB, dtype=jnp.int32)[:, None, None]).astype(jnp.bfloat16)
    same_doc = query_seg[:, None] == segment_row[None, :]
    return (one_hot, same_doc)


def block_scores(query_block, key_rows, table_local, one_hot, same_doc):
    attention_scores = jnp.einsum(
        "ihd,jhd->hij", query_block, key_rows, preferred_element_type=jnp.float32
    )
    attention_scores = attention_scores + jnp.einsum(
        "bij,bh->hij", one_hot, table_local, preferred_element_type=jnp.float32
    )
    return jnp.where(same_doc[None], attention_scores, MASKED)


def layer_forward(tokens, small_set, attn_set, ffn_set, segment_row, position_row):
    attn_gain, ffn_gain, table_flat = small_set
    w_query, w_key, w_value, w_attn_out = attn_set
    w_gate, w_up, w_down = ffn_set
    heads_here = w_query.shape[1] // DH
    head_start = lax.axis_index("ctx") * heads_here
    table_local = lax.dynamic_slice_in_dim(table_flat.reshape(NB, H), head_start, heads_here, 1)
    normalized_rows, attn_back = jax.vjp(rms_norm, tokens, attn_gain.astype(jnp.float32))
    normed_rows = lax.all_gather(normalized_rows.astype(jnp.bfloat16), "ctx", axis=0, tiled=True)
    seq_len = normed_rows.shape[0]
    queries = (
        jnp.dot(normed_rows, w_query, preferred_element_type=jnp.float32)
        .astype(jnp.bfloat16)
        .reshape(seq_len, heads_here, DH)
    )
    key_rows = (
        jnp.dot(normed_rows, w_key, preferred_element_type=jnp.float32)
        .astype(jnp.bfloat16)
        .reshape(seq_len, heads_here, DH)
    )
    value_rows = (
        jnp.dot(normed_rows, w_value, preferred_element_type=jnp.float32)
        .astype(jnp.bfloat16)
        .reshape(seq_len, heads_here, DH)
    )
    starts = jnp.arange(seq_len // QB, dtype=jnp.int32) * QB

    def forward_block(start):
        one_hot, same_doc = block_masks(segment_row, position_row, start)
        query_block = lax.dynamic_slice_in_dim(queries, start, QB, 0)
        attention_scores = block_scores(query_block, key_rows, table_local, one_hot, same_doc)
        row_peak = jnp.max(attention_scores, axis=-1, keepdims=True)
        lifted = jnp.exp(attention_scores - row_peak)
        row_total = jnp.sum(lifted, axis=-1, keepdims=True)
        prob_low = (lifted / row_total).astype(jnp.bfloat16)
        attended_part = jnp.einsum(
            "hij,jhd->ihd", prob_low, value_rows, preferred_element_type=jnp.float32
        )
        return (attended_part, row_peak + jnp.log(row_total))

    attended, log_total = lax.map(forward_block, starts)
    attended_low = attended.reshape(seq_len, heads_here * DH).astype(jnp.bfloat16)
    attn_term = jnp.dot(attended_low, w_attn_out, preferred_element_type=jnp.float32)
    residual = tokens + lax.psum_scatter(attn_term, "ctx", scatter_dimension=0, tiled=True)
    normed_ffn, ffn_back = jax.vjp(rms_norm, residual, ffn_gain.astype(jnp.float32))
    ffn_rows = lax.all_gather(normed_ffn.astype(jnp.bfloat16), "ctx", axis=0, tiled=True)
    gate_value = jnp.dot(ffn_rows, w_gate, preferred_element_type=jnp.float32)
    up_value = jnp.dot(ffn_rows, w_up, preferred_element_type=jnp.float32)
    gelu_gate, gelu_back = jax.vjp(gelu_tanh, gate_value)
    ffn_hidden = (gelu_gate * up_value).astype(jnp.bfloat16)
    down_term = jnp.dot(ffn_hidden, w_down, preferred_element_type=jnp.float32)
    result = residual + lax.psum_scatter(
        down_term.astype(jnp.bfloat16), "ctx", scatter_dimension=0, tiled=True
    ).astype(jnp.float32)
    stored = (
        attn_back,
        normed_rows,
        queries,
        key_rows,
        value_rows,
        table_local,
        head_start,
        starts,
        log_total,
        attended_low,
        ffn_back,
        ffn_rows,
        up_value,
        gelu_gate,
        gelu_back,
        ffn_hidden,
    )
    return (result, stored)


def on_device(
    hidden,
    segment_ids,
    positions,
    attn_gain,
    w_query,
    w_key,
    w_value,
    w_attn_out,
    rel_table,
    ffn_gain,
    w_gate,
    w_up,
    w_down,
    cotangent,
):
    tokens = hidden[0].astype(jnp.float32)
    segment_row = segment_ids[0]
    position_row = positions[0]
    small_set = (
        lax.all_gather(attn_gain, ("dp", "ctx", "fsdp"), axis=0, tiled=True),
        lax.all_gather(ffn_gain, ("dp", "ctx", "fsdp"), axis=0, tiled=True),
        lax.all_gather(rel_table, ("dp", "ctx", "fsdp"), axis=0, tiled=True),
    )
    attn_set = gather_attention(w_query, w_key, w_value, w_attn_out)
    ffn_set = gather_feedforward(w_gate, w_up, w_down)
    result, unused_stored = layer_forward(
        tokens, small_set, attn_set, ffn_set, segment_row, position_row
    )
    back_attn = gather_attention(w_query, w_key, w_value, w_attn_out)
    back_ffn = gather_feedforward(w_gate, w_up, w_down)
    recomputed, stored = layer_forward(
        tokens, small_set, back_attn, back_ffn, segment_row, position_row
    )
    (
        attn_back,
        normed_rows,
        queries,
        key_rows,
        value_rows,
        table_local,
        head_start,
        starts,
        log_total,
        attended_low,
        ffn_back,
        ffn_rows,
        up_value,
        gelu_gate,
        gelu_back,
        ffn_hidden,
    ) = stored
    full_query, full_key, full_value, full_attn_out = back_attn
    full_gate, full_up, full_down = back_ffn
    seq_len = normed_rows.shape[0]
    heads_here = queries.shape[1]
    grad_rows = lax.all_gather(cotangent[0], "ctx", axis=0, tiled=True)
    grad_w_down = jnp.einsum("tf,td->fd", ffn_hidden, grad_rows, preferred_element_type=jnp.float32)
    grad_hidden_ffn = jnp.einsum(
        "td,fd->tf", grad_rows, full_down, preferred_element_type=jnp.float32
    )
    up_value_gradient = (grad_hidden_ffn * gelu_gate).astype(jnp.bfloat16)
    grad_gate_value = gelu_back(grad_hidden_ffn * up_value)[0].astype(jnp.bfloat16)
    grad_w_gate = jnp.einsum(
        "td,tf->df", ffn_rows, grad_gate_value, preferred_element_type=jnp.float32
    )
    grad_w_up = jnp.einsum(
        "td,tf->df", ffn_rows, up_value_gradient, preferred_element_type=jnp.float32
    )
    ffn_normed_term = jnp.einsum(
        "tf,df->td", grad_gate_value, full_gate, preferred_element_type=jnp.float32
    )
    ffn_normed_term = ffn_normed_term + jnp.einsum(
        "tf,df->td", up_value_gradient, full_up, preferred_element_type=jnp.float32
    )
    grad_normed_ffn = lax.psum_scatter(ffn_normed_term, "ctx", scatter_dimension=0, tiled=True)
    grad_residual_norm, grad_ffn_gain = ffn_back(grad_normed_ffn)
    grad_residual = cotangent[0].astype(jnp.float32) + grad_residual_norm
    ffn_sums = (
        lax.psum_scatter(
            grad_w_gate.astype(jnp.bfloat16), ("dp", "fsdp"), scatter_dimension=0, tiled=True
        ).astype(jnp.float32),
        lax.psum_scatter(
            grad_w_up.astype(jnp.bfloat16), ("dp", "fsdp"), scatter_dimension=0, tiled=True
        ).astype(jnp.float32),
        lax.psum_scatter(
            grad_w_down.astype(jnp.bfloat16), ("dp", "fsdp"), scatter_dimension=1, tiled=True
        ).astype(jnp.float32),
    )
    branch_rows = lax.all_gather(grad_residual.astype(jnp.bfloat16), "ctx", axis=0, tiled=True)
    grad_w_attn_out = jnp.einsum(
        "ti,td->id", attended_low, branch_rows, preferred_element_type=jnp.float32
    )
    grad_attended = jnp.einsum(
        "td,id->ti", branch_rows, full_attn_out, preferred_element_type=jnp.float32
    )
    grad_attended = grad_attended.astype(jnp.bfloat16).reshape(seq_len, heads_here, DH)

    def backward_block(operands):
        start, block_total = operands
        one_hot, same_doc = block_masks(segment_row, position_row, start)
        query_block = lax.dynamic_slice_in_dim(queries, start, QB, 0)
        grad_part = lax.dynamic_slice_in_dim(grad_attended, start, QB, 0)
        attention_scores = block_scores(query_block, key_rows, table_local, one_hot, same_doc)
        weights = jnp.exp(attention_scores - block_total)
        prob_low = weights.astype(jnp.bfloat16)
        grad_probs = jnp.einsum(
            "ihd,jhd->hij", grad_part, value_rows, preferred_element_type=jnp.float32
        )
        centred = grad_probs - jnp.sum(weights * grad_probs, axis=-1, keepdims=True)
        grad_scores = (weights * centred).astype(jnp.bfloat16)
        grad_query_part = jnp.einsum(
            "hij,jhd->ihd", grad_scores, key_rows, preferred_element_type=jnp.float32
        )
        grad_key_part = jnp.einsum(
            "hij,ihd->jhd", grad_scores, query_block, preferred_element_type=jnp.float32
        )
        grad_value_part = jnp.einsum(
            "hij,ihd->jhd", prob_low, grad_part, preferred_element_type=jnp.float32
        )
        grad_bias_part = jnp.einsum(
            "hij,bij->bh", grad_scores, one_hot, preferred_element_type=jnp.float32
        )
        return (grad_query_part, grad_key_part, grad_value_part, grad_bias_part)

    query_blocks, key_blocks, value_blocks, bias_blocks = lax.map(
        backward_block, (starts, log_total)
    )
    grad_queries_low = query_blocks.reshape(seq_len, heads_here * DH).astype(jnp.bfloat16)
    grad_keys_low = (
        jnp.sum(key_blocks, axis=0).reshape(seq_len, heads_here * DH).astype(jnp.bfloat16)
    )
    grad_values_low = (
        jnp.sum(value_blocks, axis=0).reshape(seq_len, heads_here * DH).astype(jnp.bfloat16)
    )
    grad_w_query = jnp.einsum(
        "td,te->de", normed_rows, grad_queries_low, preferred_element_type=jnp.float32
    )
    grad_w_key = jnp.einsum(
        "td,te->de", normed_rows, grad_keys_low, preferred_element_type=jnp.float32
    )
    grad_w_value = jnp.einsum(
        "td,te->de", normed_rows, grad_values_low, preferred_element_type=jnp.float32
    )
    normed_term = jnp.einsum(
        "te,de->td", grad_queries_low, full_query, preferred_element_type=jnp.float32
    )
    normed_term = normed_term + jnp.einsum(
        "te,de->td", grad_keys_low, full_key, preferred_element_type=jnp.float32
    )
    normed_term = normed_term + jnp.einsum(
        "te,de->td", grad_values_low, full_value, preferred_element_type=jnp.float32
    )
    grad_normed = lax.psum_scatter(
        normed_term.astype(jnp.bfloat16), "ctx", scatter_dimension=0, tiled=True
    ).astype(jnp.float32)
    token_norm_gradient, grad_attn_gain = attn_back(grad_normed)
    grad_tokens = grad_residual + token_norm_gradient
    attn_sums = (
        lax.psum_scatter(
            grad_w_query.astype(jnp.bfloat16), ("dp", "fsdp"), scatter_dimension=0, tiled=True
        ).astype(jnp.float32),
        lax.psum_scatter(
            grad_w_key.astype(jnp.bfloat16), ("dp", "fsdp"), scatter_dimension=0, tiled=True
        ).astype(jnp.float32),
        lax.psum_scatter(
            grad_w_value.astype(jnp.bfloat16), ("dp", "fsdp"), scatter_dimension=0, tiled=True
        ).astype(jnp.float32),
        lax.psum_scatter(
            grad_w_attn_out.astype(jnp.bfloat16), ("dp", "fsdp"), scatter_dimension=1, tiled=True
        ).astype(jnp.float32),
    )
    bias_sum = jnp.sum(bias_blocks, axis=0)
    table_term = lax.dynamic_update_slice(
        jnp.zeros((NB, H), jnp.float32), bias_sum, (jnp.int32(0), head_start)
    )
    small_sums = (
        lax.psum_scatter(grad_attn_gain, ("dp", "ctx", "fsdp"), scatter_dimension=0, tiled=True),
        lax.psum_scatter(grad_ffn_gain, ("dp", "ctx", "fsdp"), scatter_dimension=0, tiled=True),
        lax.psum_scatter(
            table_term.reshape(NB * H), ("dp", "ctx", "fsdp"), scatter_dimension=0, tiled=True
        ),
    )
    return (
        result[None].astype(jnp.bfloat16),
        grad_tokens[None],
        small_sums[0],
        attn_sums[0],
        attn_sums[1],
        attn_sums[2],
        attn_sums[3],
        small_sums[2],
        small_sums[1],
        ffn_sums[0],
        ffn_sums[1],
        ffn_sums[2],
    )


def solution(mesh):
    in_specs = (
        P(("dp", "fsdp"), "ctx", None),
        P(("dp", "fsdp"), None),
        P(("dp", "fsdp"), None),
        P(("dp", "ctx", "fsdp")),
        P(("dp", "fsdp"), "ctx"),
        P(("dp", "fsdp"), "ctx"),
        P(("dp", "fsdp"), "ctx"),
        P("ctx", ("dp", "fsdp")),
        P(("dp", "ctx", "fsdp")),
        P(("dp", "ctx", "fsdp")),
        P(("dp", "fsdp"), "ctx"),
        P(("dp", "fsdp"), "ctx"),
        P("ctx", ("dp", "fsdp")),
        P(("dp", "fsdp"), "ctx", None),
    )
    out_specs = (
        P(("dp", "fsdp"), "ctx", None),
        P(("dp", "fsdp"), "ctx", None),
        P(("dp", "ctx", "fsdp")),
        P(("dp", "fsdp"), "ctx"),
        P(("dp", "fsdp"), "ctx"),
        P(("dp", "fsdp"), "ctx"),
        P("ctx", ("dp", "fsdp")),
        P(("dp", "ctx", "fsdp")),
        P(("dp", "ctx", "fsdp")),
        P(("dp", "fsdp"), "ctx"),
        P(("dp", "fsdp"), "ctx"),
        P("ctx", ("dp", "fsdp")),
    )
    return jax.shard_map(
        on_device, mesh=mesh, in_specs=in_specs, out_specs=out_specs, check_vma=False
    )
```

profile of v0, /device:TPU:0, one launch (start us, length us, event | category | flops | bytes accessed | tf_op | source)
XLA Modules:
  0.0 1926.7 jit_solution(9889861834597921747)
XLA Ops:
  10.6 43.6 %all-reduce.8 = (bf16[2048]{0:T(1024)(128)(2,1)}, bf16[2048]{0:T(1024)(128)(2,1)S(1)}, bf16[32,32]{1,0:T(8,128)(2,1)S(1)}) all-reduce(bf16[2048]{0:T(1024)(128)(2,1)S(1)} %dynamic-update-slice.2, bf16[2048]{0:T(1024)(128)(2,1)S(1)} %dynamic-update-slice, ...), channel_id=1, replica_groups=mesh['dp'=4,'ctx'=4,'fsdp'=2] {'dp','ctx','fsdp'}, use_global_device_ids=true, to_apply=%add.2 | all-reduce | flops 5120 | bytes 20480
  63.3 35.1 %all-gather.14.cloned.1.call-done = bf16[1024,2048]{1,0:T(8,128)(2,1)} async-done(((bf16[256,2048]{1,0:T(8,128)(2,1)}), bf16[1024,2048]{1,0:T(8,128)(2,1)}) %all-gather.14.cloned.1.call-update) | async-done | bytes 4194320 | tf_op jit(solution)/shard_map/all_gather | solution.py:79
  104.7 45.3 %all-gather.18.cloned.1.call-done = bf16[2048,512]{1,0:T(8,128)(2,1)} async-done(((bf16[256,512]{1,0:T(8,128)(2,1)}), bf16[2048,512]{1,0:T(8,128)(2,1)}) %all-gather.18.cloned.1.call-update) | async-done | bytes 2097168 | tf_op jit(solution)/shard_map/all_gather | solution.py:38
  156.1 43.6 %all-gather.16.cloned.1.call-done = bf16[2048,512]{1,0:T(8,128)(2,1)} async-done(((bf16[256,512]{1,0:T(8,128)(2,1)}), bf16[2048,512]{1,0:T(8,128)(2,1)}) %all-gather.16.cloned.1.call-update) | async-done | bytes 2097168 | tf_op jit(solution)/shard_map/all_gather | solution.py:37
  206.1 128.6 %while.39 = (s32[]{:T(128)}, bf16[2,512,8,64]{1,3,2,0:T(8,128)(2,1)S(1)}, f32[2,8,512,1]{2,1,3,0:T(8,128)S(1)}, s32[2]{0:T(128)S(1)}, s32[1024]{0:T(1024)S(1)}, ...) while((s32[]{:T(128)}, ...), condition=%wide.region_11.12_spmd, body=%wide.region_8.11_spmd.sunk | while | flops 1407709184 | bytes 160060144 | solution.py:111
  344.5 69.5 %reduce-scatter.17.cloned.1.call-done = f32[256,2048]{1,0:T(8,128)} async-done(((f32[1024,2048]{1,0:T(8,128)}), f32[256,2048]{1,0:T(8,128)}) %reduce-scatter.17.cloned.1.call-update) | async-done | bytes 2097168 | tf_op jit(solution)/shard_map/reduce_scatter | solution.py:114
  419.9 142.7 %while.38 = (s32[]{:T(128)}, bf16[2,512,8,64]{1,3,2,0:T(8,128)(2,1)S(1)}, s32[2]{0:T(128)S(1)}, s32[1024]{0:T(1024)S(1)}, s32[1,1024]{1,0:T(1,128)S(1)}, /*index...) while((s32[]{:T(128)}, ...), condition=%wide.region_4.5_spmd, body=%wide.region_1.4_spmd.sunk | while | flops 1403525120 | bytes 109630152 | solution.py:111
  580.3 46.1 %all-gather.26.cloned.1.call-done = bf16[2048,1280]{1,0:T(8,128)(2,1)} async-done(((bf16[256,1280]{1,0:T(8,128)(2,1)}), bf16[2048,1280]{1,0:T(8,128)(2,1)}) %all-gather.26.cloned.1.call-update) | async-done | bytes 5242896 | tf_op jit(solution)/shard_map/all_gather | solution.py:46
  660.6 89.5 %all-gather.30.cloned.1.call-done = bf16[1280,2048]{1,0:T(8,128)(2,1)} async-done(((bf16[1280,256]{1,0:T(8,128)(2,1)}), bf16[1280,2048]{1,0:T(8,128)(2,1)}) %all-gather.30.cloned.1.call-update) | async-done | bytes 5242896 | tf_op jit(solution)/shard_map/all_gather | solution.py:48
  782.9 39.8 %reduce-scatter.13.cloned.1.call-done = f32[256,2048]{1,0:T(8,128)} async-done(((f32[1024,2048]{1,0:T(8,128)}), f32[256,2048]{1,0:T(8,128)}) %reduce-scatter.13.cloned.1.call-update) | async-done | bytes 2097168 | tf_op jit(solution)/shard_map/reduce_scatter | solution.py:114
  822.7 74.3 %reduce-scatter.19.cloned.1.call-done = f32[256,2048]{1,0:T(8,128)} async-done(((f32[1024,2048]{1,0:T(8,128)}), f32[256,2048]{1,0:T(8,128)}) %reduce-scatter.19.cloned.1.call-update) | async-done | bytes 2097168 | tf_op jit(solution)/shard_map/reduce_scatter | solution.py:221
  902.9 34.5 %all-gather.34.cloned.1.call-done = bf16[1024,2048]{1,0:T(8,128)(2,1)} async-done(((bf16[256,2048]{1,0:T(8,128)(2,1)}), bf16[1024,2048]{1,0:T(8,128)(2,1)}) %all-gather.34.cloned.1.call-update) | async-done | bytes 4194320 | tf_op jit(solution)/shard_map/all_gather | solution.py:235
  944.8 214.2 %while.40 = (s32[]{:T(128)}, bf16[2,512,8,64]{1,3,2,0:T(8,128)(2,1)}, f32[2,1024,8,64]{1,3,2,0:T(8,128)}, f32[2,1024,8,64]{1,3,2,0:T(8,128)}, f32[2,32,8]{1,2,0:...) while((s32[]{:T(128)}, ...), condition=%wide.region_18.19_spmd, body=%wide.region_16.18_spmd.sunk | while | flops 3307728896 | bytes 294757248 | solution.py:271
  990.7 25.9 %multiply_reduce_fusion.6 = (f32[8,512]{1,0:T(8,128)S(1)}, f32[8,512,1024]{2,1,0:T(8,128)}) fusion(f32[8,512,1024]{2,1,0:T(8,128)} %fusion.240, f32[8,512]{1,0:T(8,128)S(1)} %dynamic-slice_bitcast_fusion.2, f32[512,1024,8]{1,2,0:T(8,128)} %fusion.242, bf16[1024,8,64]{0,2,1:T(8,128)(2,1)} %get-tuple-element.817, ...), kind=kOutput, calls=%fused_computation.64.clone.1 | convolution fusion | flops 557838336 | bytes 52461572 | tf_op jit(solution)/shard_map/while/body/eval_jaxpr/ihd,jhd->hij/dot_general | solution.py:62
  1085.0 25.9 %multiply_reduce_fusion.6 = (f32[8,512]{1,0:T(8,128)S(1)}, f32[8,512,1024]{2,1,0:T(8,128)}) fusion(f32[8,512,1024]{2,1,0:T(8,128)} %fusion.240, f32[8,512]{1,0:T(8,128)S(1)} %dynamic-slice_bitcast_fusion.2, f32[512,1024,8]{1,2,0:T(8,128)} %fusion.242, bf16[1024,8,64]{0,2,1:T(8,128)(2,1)} %get-tuple-element.817, ...), kind=kOutput, calls=%fused_computation.64.clone.1 | convolution fusion | flops 557838336 | bytes 52461572 | tf_op jit(solution)/shard_map/while/body/eval_jaxpr/ihd,jhd->hij/dot_general | solution.py:62
  1182.4 44.0 %reduce-scatter.21.cloned.1.call-done = bf16[256,2048]{1,0:T(8,128)(2,1)} async-done(((bf16[1024,2048]{1,0:T(8,128)(2,1)}), bf16[256,2048]{1,0:T(8,128)(2,1)}) %reduce-scatter.21.cloned.1.call-update) | async-done | bytes 1048592 | tf_op jit(solution)/shard_map/reduce_scatter | solution.py:299
  1322.5 53.3 %reduce-scatter.35.cloned.1.call-done = bf16[1280,256]{1,0:T(8,128)(2,1)} async-done(((bf16[1280,2048]{1,0:T(8,128)(2,1)}), bf16[1280,256]{1,0:T(8,128)(2,1)}) %reduce-scatter.35.cloned.1.call-update) | async-done | bytes 655376 | tf_op jit(solution)/shard_map/reduce_scatter | solution.py:231
  1378.1 103.7 %reduce-scatter.33.cloned.1.call-done = bf16[256,1280]{1,0:T(8,128)(2,1)} async-done(((bf16[2048,1280]{1,0:T(8,128)(2,1)}), bf16[256,1280]{1,0:T(8,128)(2,1)}) %reduce-scatter.33.cloned.1.call-update) | async-done | bytes 655376 | tf_op jit(solution)/shard_map/reduce_scatter | solution.py:228
  1484.0 103.9 %reduce-scatter.31.cloned.1.call-done = bf16[256,1280]{1,0:T(8,128)(2,1)} async-done(((bf16[2048,1280]{1,0:T(8,128)(2,1)}), bf16[256,1280]{1,0:T(8,128)(2,1)}) %reduce-scatter.31.cloned.1.call-update) | async-done | bytes 655376 | tf_op jit(solution)/shard_map/reduce_scatter | solution.py:225
  1590.5 68.9 %reduce-scatter.29.cloned.1.call-done = bf16[512,256]{1,0:T(8,128)(2,1)} async-done(((bf16[512,2048]{1,0:T(8,128)(2,1)}), bf16[512,256]{1,0:T(8,128)(2,1)}) %reduce-scatter.29.cloned.1.call-update) | async-done | bytes 262160 | tf_op jit(solution)/shard_map/reduce_scatter | solution.py:314
  1661.2 68.5 %reduce-scatter.23.cloned.1.call-done = bf16[256,512]{1,0:T(8,128)(2,1)} async-done(((bf16[2048,512]{1,0:T(8,128)(2,1)}), bf16[256,512]{1,0:T(8,128)(2,1)}) %reduce-scatter.23.cloned.1.call-update) | async-done | bytes 262160 | tf_op jit(solution)/shard_map/reduce_scatter | solution.py:305
  1731.5 68.5 %reduce-scatter.27.cloned.1.call-done = bf16[256,512]{1,0:T(8,128)(2,1)} async-done(((bf16[2048,512]{1,0:T(8,128)(2,1)}), bf16[256,512]{1,0:T(8,128)(2,1)}) %reduce-scatter.27.cloned.1.call-update) | async-done | bytes 262160 | tf_op jit(solution)/shard_map/reduce_scatter | solution.py:311
  1801.8 68.6 %reduce-scatter.25.cloned.1.call-done = bf16[256,512]{1,0:T(8,128)(2,1)} async-done(((bf16[2048,512]{1,0:T(8,128)(2,1)}), bf16[256,512]{1,0:T(8,128)(2,1)}) %reduce-scatter.25.cloned.1.call-update) | async-done | bytes 262160 | tf_op jit(solution)/shard_map/reduce_scatter | solution.py:308
  1872.2 40.0 %all-reduce.7 = (f32[2048]{0:T(1024)S(1)}, f32[1024]{0:T(1024)S(1)}, f32[2048]{0:T(1024)S(1)}) all-reduce(f32[2048]{0:T(1024)S(1)} %get-tuple-element.343, f32[1024]{0:T(1024)S(1)} %reshape.387, f32[2048]{0:T(1024)S(1)} %copy-done.31), channel_id=8, replica_groups=mesh['dp'=4,'ctx'=4,'fsdp'=2] {'dp','ctx','fsdp'}, use_global_device_ids=true, to_apply=%region_24.25.clone | all-reduce | flops 5120 | bytes 40960
  (310 shorter events, 665.7 us)
Async XLA Ops:
  7.2 56.2 %all-gather.20.cloned.1.call-start = ((), (), s32[]{:S(2)}) async-start(), calls=%async_computation.15 | async-start | bytes 2359296 | tf_op jit(solution)/shard_map/all_gather | solution.py:39
  7.9 90.6 %all-gather.14.cloned.1.call-start = ((), (), s32[]{:S(2)}) async-start(), calls=%async_computation.12 | async-start | bytes 5242880 | tf_op jit(solution)/shard_map/all_gather | solution.py:79
  59.4 90.5 %all-gather.18.cloned.1.call-start = ((), (), s32[]{:S(2)}) async-start(), calls=%async_computation.14 | async-start | bytes 2359296 | tf_op jit(solution)/shard_map/all_gather | solution.py:38
  60.1 139.6 %all-gather.16.cloned.1.call-start = ((), (), s32[]{:S(2)}) async-start(), calls=%async_computation.13 | async-start | bytes 2359296 | tf_op jit(solution)/shard_map/all_gather | solution.py:37
  60.7 275.3 %all-gather.22.cloned.1.call-start = ((), (), s32[]{:S(2)}) async-start(), calls=%async_computation.16 | async-start | bytes 2359296 | tf_op jit(solution)/shard_map/all_gather | solution.py:40
  61.3 352.7 %reduce-scatter.17.cloned.1.call-start = ((), (), s32[]{:S(2)}) async-start(), calls=%async_computation.23 | async-start | bytes 10485760 | tf_op jit(solution)/shard_map/reduce_scatter | solution.py:114
  343.7 226.2 %all-gather.28.cloned.1.call-start = ((), (), s32[]{:S(2)}) async-start(), calls=%async_computation.20 | async-start | bytes 5898240 | tf_op jit(solution)/shard_map/all_gather | solution.py:47
  344.5 225.5 %all-gather.32.cloned.1.call-start = ((), (), s32[]{:S(2)}) async-start(), calls=%async_computation.24 | async-start | bytes 5242880 | tf_op jit(solution)/shard_map/all_gather | solution.py:116
  417.7 208.8 %all-gather.26.cloned.1.call-start = ((), (), s32[]{:S(2)}) async-start(), calls=%async_computation.19 | async-start | bytes 5898240 | tf_op jit(solution)/shard_map/all_gather | solution.py:46
  418.4 242.2 %all-gather.36.cloned.1.call-start = ((), (), s32[]{:S(2)}) async-start(), calls=%async_computation.35 | async-start | bytes 5242880 | tf_op jit(solution)/shard_map/all_gather | solution.py:202
  419.0 331.1 %all-gather.30.cloned.1.call-start = ((), (), s32[]{:S(2)}) async-start(), calls=%async_computation.21 | async-start | bytes 5898240 | tf_op jit(solution)/shard_map/all_gather | solution.py:48
  419.7 403.0 %reduce-scatter.13.cloned.1.call-start = ((), (), s32[]{:S(2)}) async-start(), calls=%async_computation.17 | async-start | bytes 10485760 | tf_op jit(solution)/shard_map/reduce_scatter | solution.py:114
  569.8 327.2 %reduce-scatter.19.cloned.1.call-start = ((), (), s32[]{:S(2)}) async-start(), calls=%async_computation.25 | async-start | bytes 10485760 | tf_op jit(solution)/shard_map/reduce_scatter | solution.py:221
  782.8 154.7 %all-gather.34.cloned.1.call-start = ((), (), s32[]{:S(2)}) async-start(), calls=%async_computation.26 | async-start | bytes 5242880 | tf_op jit(solution)/shard_map/all_gather | solution.py:235
  902.9 323.5 %reduce-scatter.21.cloned.1.call-start = ((), (), s32[]{:S(2)}) async-start(), calls=%async_computation.27 | async-start | bytes 5242880 | tf_op jit(solution)/shard_map/reduce_scatter | solution.py:299
  1181.8 110.3 %all-gather.24.cloned.1.call-start = ((), (), s32[]{:S(2)}) async-start(), calls=%async_computation.18 | async-start | bytes 5242880 | tf_op jit(solution)/shard_map/all_gather | solution.py:116
  1234.7 141.1 %reduce-scatter.35.cloned.1.call-start = ((), (), s32[]{:S(2)}) async-start(), calls=%async_computation.34 | async-start | bytes 5898240 | tf_op jit(solution)/shard_map/reduce_scatter | solution.py:231
  1246.5 235.3 %reduce-scatter.33.cloned.1.call-start = ((), (), s32[]{:S(2)}) async-start(), calls=%async_computation.33 | async-start | bytes 5898240 | tf_op jit(solution)/shard_map/reduce_scatter | solution.py:228
  1256.4 331.5 %reduce-scatter.31.cloned.1.call-start = ((), (), s32[]{:S(2)}) async-start(), calls=%async_computation.32 | async-start | bytes 5898240 | tf_op jit(solution)/shard_map/reduce_scatter | solution.py:225
  1266.3 393.1 %reduce-scatter.29.cloned.1.call-start = ((), (), s32[]{:S(2)}) async-start(), calls=%async_computation.31 | async-start | bytes 2359296 | tf_op jit(solution)/shard_map/reduce_scatter | solution.py:314
  1273.4 456.3 %reduce-scatter.23.cloned.1.call-start = ((), (), s32[]{:S(2)}) async-start(), calls=%async_computation.28 | async-start | bytes 2359296 | tf_op jit(solution)/shard_map/reduce_scatter | solution.py:305
  1279.5 520.4 %reduce-scatter.27.cloned.1.call-start = ((), (), s32[]{:S(2)}) async-start(), calls=%async_computation.30 | async-start | bytes 2359296 | tf_op jit(solution)/shard_map/reduce_scatter | solution.py:311
  1285.8 584.6 %reduce-scatter.25.cloned.1.call-start = ((), (), s32[]{:S(2)}) async-start(), calls=%async_computation.29 | async-start | bytes 2359296 | tf_op jit(solution)/shard_map/reduce_scatter | solution.py:308
  1291.8 625.1 %reduce-scatter.15.cloned.1.call-start = ((), (), s32[]{:S(2)}) async-start(), calls=%async_computation.22 | async-start | bytes 5242880 | tf_op jit(solution)/shard_map/reduce_scatter | solution.py:122
  (56 other events, 2583.4 us)
Sparse Core Ops, SparseCore 0:
  10.1 53.1 all-gather.19
  65.5 32.9 all-gather.13
  100.6 49.2 all-gather.17
  151.9 47.7 all-gather.15
  201.6 49.5 all-gather.21
  343.8 70.1 reduce-scatter.16
  416.5 86.3 all-gather.27
  505.1 32.5 all-gather.31
  540.1 86.2 all-gather.25
  627.9 32.6 all-gather.35
  662.9 87.2 all-gather.29
  752.7 69.9 reduce-scatter.12
  825.3 71.7 reduce-scatter.18
  903.0 34.4 all-gather.33
  1181.9 44.4 reduce-scatter.20
  1234.9 34.4 all-gather.23
  1272.8 102.9 reduce-scatter.34
  1379.3 102.4 reduce-scatter.32
  1485.4 102.4 reduce-scatter.30
  1591.3 68.0 reduce-scatter.28
  1662.9 66.7 reduce-scatter.22
  1733.2 66.7 reduce-scatter.26
  1803.5 66.8 reduce-scatter.24
  1872.8 44.1 reduce-scatter.14
where the time goes:
time: 1930 us
  waiting for transfers between devices  1090 us (56%)
  matrix products  520 us (27%)
  other arithmetic  126 us (7%)
  blocking collectives  83.6 us (4%)
  loops' own time  53 us (3%)
  local copies, waits for them, and re-layouts  36.1 us (2%)
    dot_general x6, matrix products, block_scores(): jnp.einsum('ihd,jhd->hij', query_block, key_rows, preferred_element_type=...  149 us
    reduce_scatter x2, waiting for transfers between devices, layer_forward(): lax.psum_scatter(attn_term, 'ctx', scatter_dimension=0, tiled=True)  109 us
    reduce_scatter x1, waiting for transfers between devices, on_device(): lax.psum_scatter(grad_w_gate.astype(jnp.bfloat16), ('dp', 'fsdp'), scatte...  104 us
    reduce_scatter x1, waiting for transfers between devices, on_device(): lax.psum_scatter(grad_w_up.astype(jnp.bfloat16), ('dp', 'fsdp'), scatter_...  104 us
    all_gather x1, waiting for transfers between devices, gather_feedforward(): lax.all_gather(w_down, ('dp', 'fsdp'), axis=1, tiled=True)  89.5 us
    unnamed x2, blocking collectives  83.6 us
    dot_general x6, matrix products, block_scores(): jnp.einsum('bij,bh->hij', one_hot, table_local, preferred_element_type=jn...  75.4 us
    reduce_scatter x1, waiting for transfers between devices, on_device(): lax.psum_scatter(ffn_normed_term, 'ctx', scatter_dimension=0, tiled=True)  74.3 us
  transfers between devices with their start and end apart: 24, of which 20 were waited for; matrix products, arithmetic and copies ran while one was open for 23% of the time, Pallas kernels for 0%

commit v1 on v0

--- a/solution.py
+++ b/solution.py
@@ -12,6 +12,19 @@
 MASKED = -1e30
 
 
+def collect(array, axis, dim):
+    count, place, rows = (lax.axis_size(axis), lax.axis_index(axis), array.shape[dim])
+    forward = [(i, (i + 1) % count) for i in range(count)]
+    out = jnp.zeros((*array.shape[:dim], count * rows, *array.shape[dim + 1 :]), array.dtype)
+    current = array
+    for hop in range(count):
+        owner = (place - hop) % count
+        out = lax.dynamic_update_slice_in_dim(out, current, owner * rows, axis=dim)
+        if hop < count - 1:
+            current = lax.ppermute(current, axis, forward)
+    return out
+
+
 def rms_norm(values, gain):
     return values * lax.rsqrt(jnp.mean(values * values, axis=-1, keepdims=True) + EPSILON) * gain
 
@@ -43,7 +56,7 @@
 
 def gather_feedforward(w_gate, w_up, w_down):
     return (
-        lax.all_gather(w_gate, ("dp", "fsdp"), axis=0, tiled=True),
+        collect(w_gate, ("dp", "fsdp"), 0),
         lax.all_gather(w_up, ("dp", "fsdp"), axis=0, tiled=True),
         lax.all_gather(w_down, ("dp", "fsdp"), axis=1, tiled=True),
     )

time: 1930 us -> 1890 us (0.979)
  waiting for transfers between devices: 1090 us -> 1030 us
    ppermute x0 -> x7, waiting for transfers between devices: none -> 142 us  [collect(): current = lax.ppermute(current, axis, forward)]
    all_gather x1, waiting for transfers between devices: 89.5 us -> 0.01 us  [gather_feedforward(): lax.all_gather(w_down, ('dp', 'fsdp'), axis=1, tiled=True)]
    all_gather x1 -> x0, waiting for transfers between devices: 46.1 us -> none  [gather_feedforward(): lax.all_gather(w_gate, ('dp', 'fsdp'), axis=0, tiled=True)]
    reduce_scatter x2, waiting for transfers between devices: 109 us -> 68.1 us  [layer_forward(): lax.psum_scatter(attn_term, 'ctx', scatter_dimension=0, tiled=True)]
    all_gather x1, waiting for transfers between devices: 23.8 us -> 0.01 us  [on_device(): grad_rows = lax.all_gather(cotangent[0], 'ctx', axis=0, tiled=True)]
  transfers between devices with their start and end apart: 24 -> 30, of which waited for: 20 -> 23; matrix products, arithmetic and copies ran while one was open for 23% -> 24% of each run, Pallas kernels for 0% -> 0%
where the time goes in v1:
time: 1890 us; the launch traced here: 1880 us
  waiting for transfers between devices  1030 us (54%)
  matrix products  521 us (28%)
  other arithmetic  126 us (7%)
  blocking collectives  83.7 us (4%)
  loops' own time  53 us (3%)
  local copies, waits for them, and re-layouts  47.8 us (3%)
    dot_general x6, matrix products, block_scores(): jnp.einsum('ihd,jhd->hij', query_block, key_rows, preferred_element_type=...  148 us
    ppermute x7, waiting for transfers between devices, collect(): current = lax.ppermute(current, axis, forward)  142 us
    reduce_scatter x1, waiting for transfers between devices, on_device(): lax.psum_scatter(grad_w_gate.astype(jnp.bfloat16), ('dp', 'fsdp'), scatte...  104 us
    reduce_scatter x1, waiting for transfers between devices, on_device(): lax.psum_scatter(grad_w_up.astype(jnp.bfloat16), ('dp', 'fsdp'), scatter_...  104 us
    unnamed x2, blocking collectives  83.7 us
    dot_general x6, matrix products, block_scores(): jnp.einsum('bij,bh->hij', one_hot, table_local, preferred_element_type=jn...  75.4 us
    reduce_scatter x1, waiting for transfers between devices, on_device(): lax.psum_scatter(ffn_normed_term, 'ctx', scatter_dimension=0, tiled=True)  71.1 us
    reduce_scatter x1, waiting for transfers between devices, on_device(): lax.psum_scatter(grad_w_attn_out.astype(jnp.bfloat16), ('dp', 'fsdp'), sc...  69 us
  transfers between devices with their start and end apart: 30, of which 23 were waited for; matrix products, arithmetic and copies ran while one was open for 24% of the time, Pallas kernels for 0%

profile of v1, /device:TPU:0, one launch (start us, length us, event | category | flops | bytes accessed | tf_op | source)
XLA Modules:
  0.0 1878.9 jit_solution(12106181103794469116)
XLA Ops:
  10.6 43.6 %all-reduce.8 = (bf16[2048]{0:T(1024)(128)(2,1)}, bf16[2048]{0:T(1024)(128)(2,1)S(1)}, bf16[32,32]{1,0:T(8,128)(2,1)S(1)}) all-reduce(bf16[2048]{0:T(1024)(128)(2,1)S(1)} %dynamic-update-slice.2, bf16[2048]{0:T(1024)(128)(2,1)S(1)} %dynamic-update-slice, ...), channel_id=1, replica_groups=mesh['dp'=4,'ctx'=4,'fsdp'=2] {'dp','ctx','fsdp'}, use_global_device_ids=true, to_apply=%add.2 | all-reduce | flops 5120 | bytes 20480
  63.3 35.1 %all-gather.13.cloned.1.call-done = bf16[1024,2048]{1,0:T(8,128)(2,1)} async-done(((bf16[256,2048]{1,0:T(8,128)(2,1)}), bf16[1024,2048]{1,0:T(8,128)(2,1)}) %all-gather.13.cloned.1.call-update) | async-done | bytes 4194320 | tf_op jit(solution)/shard_map/all_gather | solution.py:92
  104.7 45.3 %all-gather.17.cloned.1.call-done = bf16[2048,512]{1,0:T(8,128)(2,1)} async-done(((bf16[256,512]{1,0:T(8,128)(2,1)}), bf16[2048,512]{1,0:T(8,128)(2,1)}) %all-gather.17.cloned.1.call-update) | async-done | bytes 2097168 | tf_op jit(solution)/shard_map/all_gather | solution.py:51
  156.1 43.6 %all-gather.15.cloned.1.call-done = bf16[2048,512]{1,0:T(8,128)(2,1)} async-done(((bf16[256,512]{1,0:T(8,128)(2,1)}), bf16[2048,512]{1,0:T(8,128)(2,1)}) %all-gather.15.cloned.1.call-update) | async-done | bytes 2097168 | tf_op jit(solution)/shard_map/all_gather | solution.py:50
  206.1 128.7 %while.39 = (s32[]{:T(128)}, bf16[2,512,8,64]{1,3,2,0:T(8,128)(2,1)S(1)}, f32[2,8,512,1]{2,1,3,0:T(8,128)S(1)}, s32[2]{0:T(128)S(1)}, s32[1024]{0:T(1024)S(1)}, ...) while((s32[]{:T(128)}, ...), condition=%wide.region_11.12_spmd, body=%wide.region_8.11_spmd.sunk | while | flops 1407709184 | bytes 160060144 | solution.py:124
  238.1 24.2 %fusion.232 = (f32[8,512]{1,0:T(8,128)S(1)}, f32[8,512,1024]{2,1,0:T(8,128)}) fusion(f32[512,1024,8]{1,2,0:T(8,128)} %fusion.231, bf16[1024,8,64]{0,2,1:T(8,128)(2,1)} %get-tuple-element.721, bf16[1024,8,64]{0,2,1:T(8,128)(2,1)} %get-tuple-element.720, s32[]{:T(128)S(6)} %select_n.180, pred[512,1024]{1,0:T(8,128)(4,1)S(1)} %broadcast_compare_fusion.7), kind=kOutput, calls=%fused_computation.192.clone.1 | convolution fusion | flops 549449728 | bytes 35667972 | tf_op jit(solution)/shard_map/while/body/eval_jaxpr/ihd,jhd->hij/dot_general | solution.py:75
  346.1 68.0 %reduce-scatter.17.cloned.1.call-done = f32[256,2048]{1,0:T(8,128)} async-done(((f32[1024,2048]{1,0:T(8,128)}), f32[256,2048]{1,0:T(8,128)}) %reduce-scatter.17.cloned.1.call-update) | async-done | bytes 2097168 | tf_op jit(solution)/shard_map/reduce_scatter | solution.py:127
  418.0 141.7 %while.38 = (s32[]{:T(128)}, bf16[2,512,8,64]{1,3,2,0:T(8,128)(2,1)S(1)}, s32[2]{0:T(128)S(1)}, s32[1024]{0:T(1024)S(1)}, s32[1,1024]{1,0:T(1,128)S(1)}, /*index...) while((s32[]{:T(128)}, ...), condition=%wide.region_4.5_spmd, body=%wide.region_1.4_spmd.sunk | while | flops 1403525120 | bytes 109630152 | solution.py:124
  592.9 33.7 %collective-permute-done.1 = bf16[256,1280]{1,0:T(8,128)(2,1)S(1)} collective-permute-done((bf16[256,1280]{1,0:T(8,128)(2,1)S(1)}, bf16[256,1280]{1,0:T(8,128)(2,1)S(1)}, u32[]{:S(2)}, u32[]{:S(2)}) %collective-permute-start.1) | collective-permute-done | bytes 655392 | tf_op jit(solution)/shard_map/ppermute | solution.py:24
  626.5 33.4 %collective-permute-done.2 = bf16[256,1280]{1,0:T(8,128)(2,1)S(1)} collective-permute-done((bf16[256,1280]{1,0:T(8,128)(2,1)S(1)}, bf16[256,1280]{1,0:T(8,128)(2,1)S(1)}, u32[]{:S(2)}, u32[]{:S(2)}) %collective-permute-start.2) | collective-permute-done | bytes 655392 | tf_op jit(solution)/shard_map/ppermute | solution.py:24
  778.3 71.1 %reduce-scatter.19.cloned.1.call-done = f32[256,2048]{1,0:T(8,128)} async-done(((f32[1024,2048]{1,0:T(8,128)}), f32[256,2048]{1,0:T(8,128)}) %reduce-scatter.19.cloned.1.call-update) | async-done | bytes 2097168 | tf_op jit(solution)/shard_map/reduce_scatter | solution.py:234
  855.3 34.5 %all-gather.31.cloned.1.call-done = bf16[1024,2048]{1,0:T(8,128)(2,1)} async-done(((bf16[256,2048]{1,0:T(8,128)(2,1)}), bf16[1024,2048]{1,0:T(8,128)(2,1)}) %all-gather.31.cloned.1.call-update) | async-done | bytes 4194320 | tf_op jit(solution)/shard_map/all_gather | solution.py:248
  897.1 214.3 %while.40 = (s32[]{:T(128)}, bf16[2,512,8,64]{1,3,2,0:T(8,128)(2,1)}, f32[2,1024,8,64]{1,3,2,0:T(8,128)}, f32[2,1024,8,64]{1,3,2,0:T(8,128)}, f32[2,32,8]{1,2,0:...) while((s32[]{:T(128)}, ...), condition=%wide.region_18.19_spmd, body=%wide.region_16.18_spmd.sunk | while | flops 3307728896 | bytes 294757248 | solution.py:284
  943.1 25.9 %multiply_reduce_fusion.6 = (f32[8,512]{1,0:T(8,128)S(1)}, f32[8,512,1024]{2,1,0:T(8,128)}) fusion(f32[8,512,1024]{2,1,0:T(8,128)} %fusion.246, f32[8,512]{1,0:T(8,128)S(1)} %dynamic-slice_bitcast_fusion.2, f32[512,1024,8]{1,2,0:T(8,128)} %fusion.248, bf16[1024,8,64]{0,2,1:T(8,128)(2,1)} %get-tuple-element.818, ...), kind=kOutput, calls=%fused_computation.64.clone.1 | convolution fusion | flops 557838336 | bytes 52461572 | tf_op jit(solution)/shard_map/while/body/eval_jaxpr/ihd,jhd->hij/dot_general | solution.py:75
  1037.4 25.9 %multiply_reduce_fusion.6 = (f32[8,512]{1,0:T(8,128)S(1)}, f32[8,512,1024]{2,1,0:T(8,128)}) fusion(f32[8,512,1024]{2,1,0:T(8,128)} %fusion.246, f32[8,512]{1,0:T(8,128)S(1)} %dynamic-slice_bitcast_fusion.2, f32[512,1024,8]{1,2,0:T(8,128)} %fusion.248, bf16[1024,8,64]{0,2,1:T(8,128)(2,1)} %get-tuple-element.818, ...), kind=kOutput, calls=%fused_computation.64.clone.1 | convolution fusion | flops 557838336 | bytes 52461572 | tf_op jit(solution)/shard_map/while/body/eval_jaxpr/ihd,jhd->hij/dot_general | solution.py:75
  1134.8 44.1 %reduce-scatter.21.cloned.1.call-done = bf16[256,2048]{1,0:T(8,128)(2,1)} async-done(((bf16[1024,2048]{1,0:T(8,128)(2,1)}), bf16[256,2048]{1,0:T(8,128)(2,1)}) %reduce-scatter.21.cloned.1.call-update) | async-done | bytes 1048592 | tf_op jit(solution)/shard_map/reduce_scatter | solution.py:312
  1275.0 53.3 %reduce-scatter.35.cloned.1.call-done = bf16[1280,256]{1,0:T(8,128)(2,1)} async-done(((bf16[1280,2048]{1,0:T(8,128)(2,1)}), bf16[1280,256]{1,0:T(8,128)(2,1)}) %reduce-scatter.35.cloned.1.call-update) | async-done | bytes 655376 | tf_op jit(solution)/shard_map/reduce_scatter | solution.py:244
  1330.5 103.7 %reduce-scatter.31.cloned.1.call-done = bf16[256,1280]{1,0:T(8,128)(2,1)} async-done(((bf16[2048,1280]{1,0:T(8,128)(2,1)}), bf16[256,1280]{1,0:T(8,128)(2,1)}) %reduce-scatter.31.cloned.1.call-update) | async-done | bytes 655376 | tf_op jit(solution)/shard_map/reduce_scatter | solution.py:238
  1436.5 103.6 %reduce-scatter.33.cloned.1.call-done = bf16[256,1280]{1,0:T(8,128)(2,1)} async-done(((bf16[2048,1280]{1,0:T(8,128)(2,1)}), bf16[256,1280]{1,0:T(8,128)(2,1)}) %reduce-scatter.33.cloned.1.call-update) | async-done | bytes 655376 | tf_op jit(solution)/shard_map/reduce_scatter | solution.py:241
  1542.6 69.0 %reduce-scatter.29.cloned.1.call-done = bf16[512,256]{1,0:T(8,128)(2,1)} async-done(((bf16[512,2048]{1,0:T(8,128)(2,1)}), bf16[512,256]{1,0:T(8,128)(2,1)}) %reduce-scatter.29.cloned.1.call-update) | async-done | bytes 262160 | tf_op jit(solution)/shard_map/reduce_scatter | solution.py:327
  1613.4 68.5 %reduce-scatter.23.cloned.1.call-done = bf16[256,512]{1,0:T(8,128)(2,1)} async-done(((bf16[2048,512]{1,0:T(8,128)(2,1)}), bf16[256,512]{1,0:T(8,128)(2,1)}) %reduce-scatter.23.cloned.1.call-update) | async-done | bytes 262160 | tf_op jit(solution)/shard_map/reduce_scatter | solution.py:318
  1683.7 68.7 %reduce-scatter.27.cloned.1.call-done = bf16[256,512]{1,0:T(8,128)(2,1)} async-done(((bf16[2048,512]{1,0:T(8,128)(2,1)}), bf16[256,512]{1,0:T(8,128)(2,1)}) %reduce-scatter.27.cloned.1.call-update) | async-done | bytes 262160 | tf_op jit(solution)/shard_map/reduce_scatter | solution.py:324
  1754.2 68.5 %reduce-scatter.25.cloned.1.call-done = bf16[256,512]{1,0:T(8,128)(2,1)} async-done(((bf16[2048,512]{1,0:T(8,128)(2,1)}), bf16[256,512]{1,0:T(8,128)(2,1)}) %reduce-scatter.25.cloned.1.call-update) | async-done | bytes 262160 | tf_op jit(solution)/shard_map/reduce_scatter | solution.py:321
  1824.5 40.1 %all-reduce.7 = (f32[2048]{0:T(1024)S(1)}, f32[1024]{0:T(1024)S(1)}, f32[2048]{0:T(1024)S(1)}) all-reduce(f32[2048]{0:T(1024)S(1)} %get-tuple-element.343, f32[1024]{0:T(1024)S(1)} %reshape.387, f32[2048]{0:T(1024)S(1)} %copy-done.34), channel_id=8, replica_groups=mesh['dp'=4,'ctx'=4,'fsdp'=2] {'dp','ctx','fsdp'}, use_global_device_ids=true, to_apply=%region_24.25.clone | all-reduce | flops 5120 | bytes 40960
  (343 shorter events, 707.1 us)
Async XLA Ops:
  7.2 56.2 %all-gather.19.cloned.1.call-start = ((), (), s32[]{:S(2)}) async-start(), calls=%async_computation.15 | async-start | bytes 2359296 | tf_op jit(solution)/shard_map/all_gather | solution.py:52
  7.9 90.6 %all-gather.13.cloned.1.call-start = ((), (), s32[]{:S(2)}) async-start(), calls=%async_computation.12 | async-start | bytes 5242880 | tf_op jit(solution)/shard_map/all_gather | solution.py:92
  59.5 90.5 %all-gather.17.cloned.1.call-start = ((), (), s32[]{:S(2)}) async-start(), calls=%async_computation.14 | async-start | bytes 2359296 | tf_op jit(solution)/shard_map/all_gather | solution.py:51
  60.2 139.5 %all-gather.15.cloned.1.call-start = ((), (), s32[]{:S(2)}) async-start(), calls=%async_computation.13 | async-start | bytes 2359296 | tf_op jit(solution)/shard_map/all_gather | solution.py:50
  60.8 275.4 %all-gather.21.cloned.1.call-start = ((), (), s32[]{:S(2)}) async-start(), calls=%async_computation.16 | async-start | bytes 2359296 | tf_op jit(solution)/shard_map/all_gather | solution.py:53
  61.4 352.8 %reduce-scatter.17.cloned.1.call-start = ((), (), s32[]{:S(2)}) async-start(), calls=%async_computation.22 | async-start | bytes 10485760 | tf_op jit(solution)/shard_map/reduce_scatter | solution.py:127
  343.8 378.9 %all-gather.33.cloned.1.call-start = ((), (), s32[]{:S(2)}) async-start(), calls=%async_computation.34 | async-start | bytes 5242880 | tf_op jit(solution)/shard_map/all_gather | solution.py:215
  344.6 378.2 %all-gather.27.cloned.1.call-start = ((), (), s32[]{:S(2)}) async-start(), calls=%async_computation.20 | async-start | bytes 5898240 | tf_op jit(solution)/shard_map/all_gather | solution.py:61
  345.3 388.0 %all-gather.25.cloned.1.call-start = ((), (), s32[]{:S(2)}) async-start(), calls=%async_computation.19 | async-start | bytes 5898240 | tf_op jit(solution)/shard_map/all_gather | solution.py:60
  346.1 387.3 %all-gather.29.cloned.1.call-start = ((), (), s32[]{:S(2)}) async-start(), calls=%async_computation.23 | async-start | bytes 5242880 | tf_op jit(solution)/shard_map/all_gather | solution.py:129
  417.8 360.5 %reduce-scatter.13.cloned.1.call-start = ((), (), s32[]{:S(2)}) async-start(), calls=%async_computation.17 | async-start | bytes 10485760 | tf_op jit(solution)/shard_map/reduce_scatter | solution.py:127
  567.0 282.4 %reduce-scatter.19.cloned.1.call-start = ((), (), s32[]{:S(2)}) async-start(), calls=%async_computation.24 | async-start | bytes 10485760 | tf_op jit(solution)/shard_map/reduce_scatter | solution.py:234
  592.9 33.7 %collective-permute-start.1 = (bf16[256,1280]{1,0:T(8,128)(2,1)S(1)}, bf16[256,1280]{1,0:T(8,128)(2,1)S(1)}, u32[]{:S(2)}, u32[]{:S(2)}) collective-permute-start(bf16[256,1280]{1,0:T(8,128)(2,1)S(1)} %collective-permute-done), channel_id=1, source_target_pairs={{0,1},{1,8},{8,9},{9,16},{16,17},{17,24},{24,25},{25,0},{2,3},{3,1... | collective-permute-start | bytes 1966088 | tf_op jit(solution)/shard_map/ppermute | solution.py:24
  778.2 111.6 %all-gather.31.cloned.1.call-start = ((), (), s32[]{:S(2)}) async-start(), calls=%async_computation.25 | async-start | bytes 5242880 | tf_op jit(solution)/shard_map/all_gather | solution.py:248
  855.2 323.6 %reduce-scatter.21.cloned.1.call-start = ((), (), s32[]{:S(2)}) async-start(), calls=%async_computation.26 | async-start | bytes 5242880 | tf_op jit(solution)/shard_map/reduce_scatter | solution.py:312
  1134.2 110.3 %all-gather.23.cloned.1.call-start = ((), (), s32[]{:S(2)}) async-start(), calls=%async_computation.18 | async-start | bytes 5242880 | tf_op jit(solution)/shard_map/all_gather | solution.py:129
  1187.2 141.1 %reduce-scatter.35.cloned.1.call-start = ((), (), s32[]{:S(2)}) async-start(), calls=%async_computation.33 | async-start | bytes 5898240 | tf_op jit(solution)/shard_map/reduce_scatter | solution.py:244
  1198.9 235.3 %reduce-scatter.31.cloned.1.call-start = ((), (), s32[]{:S(2)}) async-start(), calls=%async_computation.31 | async-start | bytes 5898240 | tf_op jit(solution)/shard_map/reduce_scatter | solution.py:238
  1208.8 331.2 %reduce-scatter.33.cloned.1.call-start = ((), (), s32[]{:S(2)}) async-start(), calls=%async_computation.32 | async-start | bytes 5898240 | tf_op jit(solution)/shard_map/reduce_scatter | solution.py:241
  1218.7 392.9 %reduce-scatter.29.cloned.1.call-start = ((), (), s32[]{:S(2)}) async-start(), calls=%async_computation.30 | async-start | bytes 2359296 | tf_op jit(solution)/shard_map/reduce_scatter | solution.py:327
  1225.8 456.1 %reduce-scatter.23.cloned.1.call-start = ((), (), s32[]{:S(2)}) async-start(), calls=%async_computation.27 | async-start | bytes 2359296 | tf_op jit(solution)/shard_map/reduce_scatter | solution.py:318
  1231.9 520.4 %reduce-scatter.27.cloned.1.call-start = ((), (), s32[]{:S(2)}) async-start(), calls=%async_computation.29 | async-start | bytes 2359296 | tf_op jit(solution)/shard_map/reduce_scatter | solution.py:324
  1238.2 584.4 %reduce-scatter.25.cloned.1.call-start = ((), (), s32[]{:S(2)}) async-start(), calls=%async_computation.28 | async-start | bytes 2359296 | tf_op jit(solution)/shard_map/reduce_scatter | solution.py:321
  1244.3 625.2 %reduce-scatter.15.cloned.1.call-start = ((), (), s32[]{:S(2)}) async-start(), calls=%async_computation.21 | async-start | bytes 5242880 | tf_op jit(solution)/shard_map/reduce_scatter | solution.py:135
  (68 other events, 2562.9 us)
Sparse Core Ops, SparseCore 0:
  10.1 53.1 all-gather.18
  65.5 32.9 all-gather.12
  100.6 49.2 all-gather.16
  151.9 47.7 all-gather.14
  201.6 49.5 all-gather.20
  344.0 70.2 reduce-scatter.16
  415.8 34.5 all-gather.32
  452.7 87.2 all-gather.26
  542.3 106.5 all-gather.24
  651.0 43.2 all-gather.28
  697.0 71.6 reduce-scatter.12
  778.3 71.0 reduce-scatter.18
  855.3 34.4 all-gather.30
  1134.3 44.5 reduce-scatter.20
  1187.3 34.4 all-gather.22
  1225.3 102.9 reduce-scatter.34
  1331.7 102.4 reduce-scatter.30
  1437.7 102.3 reduce-scatter.32
  1543.6 68.0 reduce-scatter.28
  1615.0 66.8 reduce-scatter.22
  1685.4 66.8 reduce-scatter.26
  1755.9 66.7 reduce-scatter.24
  1825.2 44.2 reduce-scatter.14
